TPU v7x, 256 devices: a whole 4x4x8 slice. The times are simulated.
256 devices in a mesh: row: 64 (over z, y, core), col: 4 (over x).
Axes of the slice: x: 4, y: 4, z: 8, core: 2. Of those that a mesh axis runs over, the one named last changes fastest.
Arguments:
- row_embed: float32 [65536, 512], P(('row', 'col')), may hold values from -1.5 to 1.5
- row_accum: float32 [65536, 512], P(('row', 'col')), may hold values from 0.001 to 0.01
- col_embed: float32 [4, 4096, 512], P('col', 'row'), may hold values from -1.5 to 1.5
- col_accum: float32 [4, 4096, 512], P('col', 'row'), may hold values from 0.001 to 0.01
- col_freq: int32 [4, 4096], P('col'), may hold values from 1000 to 29999
- row_freq: int32 [65536], P('row'), may hold values from 1000 to 29999
- block_cols: int32 [64, 4, 2], P('row', 'col'), may hold values from 0 to 3, all different within a row
- counts: int32 [64, 4, 2, 1024, 1024], P('row', 'col'), may hold values from 0 to 1024
- excluded: int32 [512], replicated, may hold values from 0 to 65535
- log_total: float32 [], replicated, may hold values from 15 to 19
Outputs:
- row_embed_new: float32 [65536, 512], P(('row', 'col'))
- row_accum_new: float32 [65536, 512], P(('row', 'col'))
- col_embed_new: float32 [4, 4096, 512], P('col', 'row')
- col_accum_new: float32 [4, 4096, 512], P('col', 'row')
Inputs may be any that keep to these rules, and one draw needn't show every extreme that they name: `block_cols`: the 2 column blocks of one row block and group are different.
All inputs are finite; a program needn't handle non-finite values.
Results may differ from a plain program's by a relative error of at most 0.0071.
The roundings to bfloat16 on the way count: a program that leaves them out, or rounds other values in their place, can miss the bound.
Values may be sent and summed in bfloat16 or wider, within the bound.
A program may use at most 128 MiB of HBM per device.

v0:
```python
import jax
import jax.numpy as jnp
from jax import lax
from jax.sharding import PartitionSpec as P

BLOCK = 1024


learn_rate = 0.2
decay_rate = 0.5


def cell_grads(count_block, predicted, row_logs, col_logs, log_total):
    nonzero = count_block > 0
    safe_count = jnp.where(nonzero, count_block.astype(jnp.float32), jnp.float32(1.0))
    baseline = log_total - row_logs[:, None] - col_logs[None, :]
    weight = 0.1 + 0.25 * jnp.sqrt(safe_count)
    fitted = weight * (predicted - baseline - jnp.log(safe_count))
    hinge_grad = jax.nn.sigmoid(predicted - baseline)
    return (jnp.where(nonzero, fitted, hinge_grad) / BLOCK).astype(jnp.bfloat16)


def body(
    row_embed,
    row_accum,
    col_embed,
    col_accum,
    col_freq,
    row_freq,
    block_cols,
    counts,
    excluded,
    log_total,
):
    block = counts.shape[3]
    slots = counts.shape[2]
    width = row_embed.shape[1]
    own_rows = row_embed.shape[0]
    own_cols = col_embed.shape[1]
    chosen = block_cols[0, 0]
    block_rows = lax.all_gather(row_embed.astype(jnp.bfloat16), "col", axis=0, tiled=True)
    piece = lax.all_gather(col_embed.astype(jnp.bfloat16), "row", axis=1, tiled=True)
    span = piece.shape[1]
    positions = jnp.arange(span, dtype=jnp.int32)
    owner_block = positions // block
    offset = positions - owner_block * block
    target = jnp.full((span,), slots * block, jnp.int32)
    for collect_slot_id in range(slots):
        target = jnp.where(
            owner_block == chosen[collect_slot_id], collect_slot_id * block + offset, target
        )
    fetched = jnp.zeros((slots * block, width), jnp.bfloat16).at[target].set(piece[0], mode="drop")
    row_logs = jnp.log(row_freq.astype(jnp.float32))
    col_logs = jnp.log(col_freq[0].astype(jnp.float32))
    row_grad = jnp.zeros((block, width), jnp.float32)
    col_parts = []
    for slot_id in range(slots):
        col_block = fetched[slot_id * block : (slot_id + 1) * block]
        block_col_logs = lax.dynamic_slice_in_dim(col_logs, chosen[slot_id] * block, block)
        predicted = lax.dot_general(
            block_rows, col_block, (((1,), (1,)), ((), ())), preferred_element_type=jnp.float32
        )
        cell = cell_grads(counts[0, 0, slot_id], predicted, row_logs, block_col_logs, log_total)
        row_grad = row_grad + jnp.dot(cell, col_block, preferred_element_type=jnp.float32)
        col_parts.append(
            lax.dot_general(
                cell, block_rows, (((0,), (0,)), ((), ())), preferred_element_type=jnp.float32
            )
        )
    positions = jnp.arange(own_cols * lax.axis_size("row"), dtype=jnp.int32)
    owner_block = positions // block
    offset = positions - owner_block * block
    summed = jnp.zeros((own_cols * lax.axis_size("row"), width), jnp.float32)
    for slot_id in range(slots):
        picked = jnp.take(col_parts[slot_id], offset, axis=0)
        summed = summed + jnp.where(
            (owner_block == chosen[slot_id])[:, None], picked, jnp.float32(0.0)
        )
    col_grad = lax.psum_scatter(summed, "row", scatter_dimension=0, tiled=True)
    own_grad = lax.psum_scatter(row_grad, "col", scatter_dimension=0, tiled=True)
    col_index = lax.axis_index("col")
    row_index = lax.axis_index("row")
    own_freq = lax.dynamic_slice_in_dim(row_freq, col_index * own_rows, own_rows).astype(
        jnp.float32
    )
    row_ids = row_index * block + col_index * own_rows + jnp.arange(own_rows, dtype=jnp.int32)
    decayed = jnp.all(row_ids[:, None] != excluded[None, :], axis=1)
    freq_root = jnp.sqrt(own_freq)
    decay_coef = jnp.where(decayed, decay_rate * freq_root / (freq_root + 30.0), jnp.float32(0.0))
    full_grad = own_grad + decay_coef[:, None] * row_embed
    row_accum_new = row_accum + full_grad * full_grad
    row_embed_new = row_embed - learn_rate * full_grad / jnp.sqrt(row_accum_new)
    col_step = col_grad[None]
    col_accum_new = col_accum + col_step * col_step
    col_embed_new = col_embed - learn_rate * col_step / jnp.sqrt(col_accum_new)
    return (row_embed_new, row_accum_new, col_embed_new, col_accum_new)


def solution(mesh):
    in_specs = (
        P(("row", "col"), None),
        P(("row", "col"), None),
        P("col", "row", None),
        P("col", "row", None),
        P("col", None),
        P("row"),
        P("row", "col", None),
        P("row", "col", None, None, None),
        P(),
        P(),
    )
    out_specs = (
        P(("row", "col"), None),
        P(("row", "col"), None),
        P("col", "row", None),
        P("col", "row", None),
    )
    return jax.shard_map(body, mesh=mesh, in_specs=in_specs, out_specs=out_specs, check_vma=False)
```

profile of v0, /device:TPU:32, one launch (start us, length us, event | category | flops | bytes accessed | tf_op | source)
XLA Modules:
  0.0 347.7 jit_solution(11396950544478308842)
XLA Ops:
  7.2 0.0 all-gather.3.cloned.1.call-start
  7.2 1.5 convert_element_type.36
  8.8 0.0 all-gather.3.cloned.1.call-update
  8.8 0.0 all-gather.5.cloned.1.call-start
  8.8 1.8 convert_element_type.37
  10.6 0.0 all-gather.5.cloned.1.call-update
  10.6 0.0 reduce-scatter.3.cloned.1.call-start
  10.7 1.3 fusion.20
  13.3 8.3 %fusion.19 = (s32[1,1,1,1024,1024]{4,3,2,1,0:T(8,128)}, s32[1,1,1,1024,1024]{4,3,2,1,0:T(8,128)}) fusion(s32[1,1,2,1024,1024]{4,3,2,1,0:T(8,128)} %param.19), kind=kLoop, calls=%fused_computation.56 | loop fusion | bytes 16777216 | tf_op jit(solution)/shard_map/slice | solution.py:63
  21.7 5.4 %copy.20 = s32[1,1,1,1024,1024]{3,4,2,1,0:T(8,128)} copy(s32[1,1,1,1024,1024]{4,3,2,1,0:T(8,128)} %get-tuple-element.10) | data formatting | bytes 8388608
  27.7 0.0 copy-start.5
  27.7 0.0 copy-start.6
  27.7 5.4 %copy.21 = s32[1,1,1,1024,1024]{3,4,2,1,0:T(8,128)} copy(s32[1,1,1,1024,1024]{4,3,2,1,0:T(8,128)} %get-tuple-element.9) | data formatting | bytes 8388608
  33.1 0.0 copy-done.5
  33.2 0.0 copy-done.6
  33.2 1.4 compare_select_fusion
  34.5 57.7 %all-gather.3.cloned.1.call-done = bf16[1,4096,512]{2,1,0:T(8,128)(2,1)} async-done(((bf16[1,64,512]{2,1,0:T(8,128)(2,1)}), bf16[1,4096,512]{2,1,0:T(8,128)(2,1)}) %all-gather.3.cloned.1.call-update) | async-done | bytes 4194320 | tf_op jit(solution)/shard_map/all_gather | solution.py:42
  92.2 19.2 %scatter_custom_fusion = bf16[2048,512]{1,0:T(8,128)(2,1)S(1)} fusion(s32[4096]{0:T(1024)S(1)} %bitcast.43, bf16[1,4096,512]{2,1,0:T(8,128)(2,1)} %all-gather.3.cloned.1.call-done, bf16[]{:T(256)} %constant.64.clone.1), kind=kCustom, calls=%fused_computation.9 | custom fusion | bytes 6291458 | tf_op jit(solution)/shard_map/scatter | solution.py:52
  111.5 7.7 %all-gather.5.cloned.1.call-done = bf16[1024,512]{1,0:T(8,128)(2,1)} async-done(((bf16[256,512]{1,0:T(8,128)(2,1)}), bf16[1024,512]{1,0:T(8,128)(2,1)}) %all-gather.5.cloned.1.call-update) | async-done | bytes 1048592 | tf_op jit(solution)/shard_map/all_gather | solution.py:41
  119.2 7.2 %multiply_convert_fusion.1 = bf16[1024,1024]{0,1:T(8,128)(2,1)S(1)} fusion(s32[1,1,1,1024,1024]{3,4,2,1,0:T(8,128)} %copy.20, bf16[1024,512]{1,0:T(8,128)(2,1)} %all-gather.5.cloned.1.call-done, f32[1024]{0:T(1024)S(1)} %bitcast.45, f32[1024]{0:T(1024)S(1)} %log_subtract_fusion, bf16[2048,512]{1,0:T(8,128)(2,1)S(1)} %scatter_custom_fusion), kind=kOutput, calls=%fused_computation.13 | convolution fusion | flops 1089470464 | bytes 8396800 | tf_op jit(solution)/shard_map/dot_general | solution.py:60
  126.4 0.0 copy-start.10
  126.4 0.0 copy-start
  126.5 0.0 copy-start.8
  126.5 1.3 fusion.6
  127.8 0.0 copy-done.10
  127.8 1.6 copy-done
  129.4 0.3 copy-done.8
  129.7 4.1 %multiply_convert_fusion = bf16[1024,1024]{0,1:T(8,128)(2,1)S(1)} fusion(s32[1,1,1,1024,1024]{3,4,2,1,0:T(8,128)S(1)} %copy-done, bf16[1024,512]{1,0:T(8,128)(2,1)S(1)} %copy-done.8, f32[1024]{0:T(1024)S(1)} %bitcast.44, f32[1024]{0:T(1024)S(1)} %log_subtract_fusion, bf16[2048,512]{1,0:T(8,128)(2,1)S(1)} %scatter_custom_fusion), kind=kOutput, calls=%fused_computation.12 | convolution fusion | flops 1089470464 | bytes 8396800 | tf_op jit(solution)/shard_map/dot_general | solution.py:60
  133.8 0.0 copy-start.9
  133.8 1.3 copy-done.9
  135.1 2.6 convolution_add_fusion
  137.7 0.0 reduce-scatter.3.cloned.1.call-update
  137.8 0.2 reduce-scatter.5.cloned.1.call-start
  138.0 1.3 fusion.12
  139.3 2.8 fusion.22
  142.2 16.8 %gather_fusion.1 = f32[4096,512]{1,0:T(8,128)} fusion(f32[1024,512]{1,0:T(8,128)S(1)} %fusion.22, s32[4096]{0:T(1024)S(1)} %fusion.17), kind=kCustom, calls=%fused_computation.1.clone | custom fusion | bytes 16793600 | tf_op jit(solution)/shard_map/jit(_take)/gather | solution.py:75
  159.0 2.9 fusion.21
  161.9 16.8 %gather_fusion = f32[4096,512]{1,0:T(8,128)} fusion(f32[1024,512]{1,0:T(8,128)S(1)} %fusion.21, s32[4096]{0:T(1024)S(1)} %fusion.17), kind=kCustom, calls=%fused_computation.clone | custom fusion | bytes 16793600 | tf_op jit(solution)/shard_map/jit(_take)/gather | solution.py:75
  178.7 9.9 %fusion = f32[4096,512]{1,0:T(8,128)} fusion(f32[4096,512]{1,0:T(8,128)} %gather_fusion.1, f32[4096,512]{1,0:T(8,128)} %gather_fusion, pred[4096]{0:T(1024)(128)(4,1)S(1)} %compare_and_fusion, pred[4096]{0:T(1024)(128)(4,1)S(1)} %get-tuple-element.15, pred[4096]{0:T(1024)(128)(4,1)S(1)} %get-tuple-element.16), kind=kLoop, calls=%fused_computation.4 | loop fusion | flops 10485760 | bytes 25178112 | tf_op jit(solution)/shard_map/add | solution.py:76
  188.6 0.0 copy-start.7
  188.6 0.0 copy-start.1
  188.6 0.0 copy-start.2
  188.6 0.0 copy-start.3
  188.6 0.0 copy-start.4
  188.6 0.0 reduce-scatter.5.cloned.1.call-update
  188.7 0.6 copy-done.7
  189.2 0.2 compare_reduce_fusion
  189.4 0.1 fusion.18
  189.5 0.0 reduce-scatter.3.cloned.1.call-done
  189.5 0.1 copy-done.1
  189.6 0.2 copy-done.2
  189.8 2.2 multiply_subtract_fusion
  192.0 147.5 %reduce-scatter.5.cloned.1.call-done = f32[64,512]{1,0:T(8,128)} async-done(((f32[4096,512]{1,0:T(8,128)}), f32[64,512]{1,0:T(8,128)}) %reduce-scatter.5.cloned.1.call-update) | async-done | bytes 131088 | tf_op jit(solution)/shard_map/reduce_scatter | solution.py:79
  339.5 0.0 copy-done.3
  339.5 0.0 copy-done.4
  339.5 1.6 fusion.9
  (6 shorter events, 0.1 us)
Async XLA Ops:
  7.2 85.1 %all-gather.3.cloned.1.call-start = ((), (), s32[]{:S(2)}) async-start(), calls=%async_computation.2 | async-start | bytes 4259840 | tf_op jit(solution)/shard_map/all_gather | solution.py:42
  8.8 110.4 %all-gather.5.cloned.1.call-start = ((), (), s32[]{:S(2)}) async-start(), calls=%async_computation.3 | async-start | bytes 1310720 | tf_op jit(solution)/shard_map/all_gather | solution.py:41
  10.6 178.9 %reduce-scatter.3.cloned.1.call-start = ((), (), s32[]{:S(2)}) async-start(), calls=%async_computation.4 | async-start | bytes 2621440 | tf_op jit(solution)/shard_map/reduce_scatter | solution.py:80
  27.7 5.4 %copy-start.5 = (s32[1,4096]{1,0:T(1,128)S(1)}, s32[1,4096]{1,0:T(1,128)}, u32[]{:S(2)}) copy-start(s32[1,4096]{1,0:T(1,128)} %param.16) | copy-start | bytes 49156
  27.7 5.4 %copy-start.6 = (s32[1024]{0:T(1024)S(1)}, s32[1024]{0:T(1024)}, u32[]{:S(2)}) copy-start(s32[1024]{0:T(1024)} %param.17) | copy-start | bytes 12292
  126.4 1.3 copy-start.10
  126.4 2.9 copy-start
  126.5 3.2 copy-start.8
  133.8 1.3 copy-start.9
  137.8 201.8 %reduce-scatter.5.cloned.1.call-start = ((), (), s32[]{:S(2)}) async-start(), calls=%async_computation.5 | async-start | bytes 8519680 | tf_op jit(solution)/shard_map/reduce_scatter | solution.py:79
  188.6 0.7 copy-start.7
  188.6 1.1 copy-start.1
  188.6 1.2 copy-start.2
  188.6 151.0 %copy-start.3 = (f32[1,64,512]{2,1,0:T(8,128)S(1)}, f32[1,64,512]{2,1,0:T(8,128)}, u32[]{:S(2)}) copy-start(f32[1,64,512]{2,1,0:T(8,128)} %param.14) | copy-start | bytes 393220
  188.6 150.9 %copy-start.4 = (f32[1,64,512]{2,1,0:T(8,128)S(1)}, f32[1,64,512]{2,1,0:T(8,128)}, u32[]{:S(2)}) copy-start(f32[1,64,512]{2,1,0:T(8,128)} %param.15) | copy-start | bytes 393220
Sparse Core Ops, SparseCore 0:
  11.3 80.8 all-gather.2
  94.6 24.5 all-gather.4
  137.9 32.5 reduce-scatter.2
  188.8 150.7 reduce-scatter.4
where the time goes:
time: 350 us; the launch traced here: 348 us
  waiting for transfers between devices  213 us (61%)
  local copies, waits for them, and re-layouts  77.4 us (22%)
  matrix products  21 us (6%)
  other arithmetic  20.1 us (6%)
  between operations  15.9 us (5%)
    reduce_scatter x1, waiting for transfers between devices, body(): col_grad = lax.psum_scatter(summed, 'row', scatter_dimension=0, tiled=True)  148 us
    all_gather x1, waiting for transfers between devices, body(): lax.all_gather(col_embed.astype(jnp.bfloat16), 'row', axis=1, tiled=True)  57.7 us
    gather x2, local copies, waits for them, and re-layouts, body(): picked = jnp.take(col_parts[slot_id], offset, axis=0)  33.6 us
    scatter x1, local copies, waits for them, and re-layouts, body(): jnp.zeros((slots * block, width), jnp.bfloat16).at[target]  19.2 us
    unnamed x24, local copies, waits for them, and re-layouts  14.9 us
    dot_general x2, matrix products, body(): lax.dot_general(block_rows, col_block, (((1,), (1,)), ((), ())), preferre...  11.4 us
    add x1, other arithmetic, body(): summed + jnp.where((owner_block == chosen[slot_id])[:, None], picked, jnp...  9.91 us
    slice x1, local copies, waits for them, and re-layouts, body(): counts[0, 0, slot_id]  8.35 us
  transfers between devices with their start and end apart: 4, of which 3 were waited for; matrix products, arithmetic and copies ran while one was open for 28% of the time, Pallas kernels for 0%

commit v1 on v0

v1 whole, which is shorter than its diff:
```python
import jax
import jax.numpy as jnp
from jax import lax
from jax.experimental import pallas as pl
from jax.experimental.pallas import tpu as pltpu
from jax.sharding import PartitionSpec as P

MESH = pl.DeviceIdType.MESH
NX, NY, NZ, NK = 4, 4, 8, 2
BLOCK = 1024
HALF = 512
PIECE = 64
QUARTER = 256
D = 512
F32 = jnp.float32
BF16 = jnp.bfloat16

learn_rate = 0.2
decay_rate = 0.5

GATHER_ORDER = (0, 2, 6, 4, 1, 7, 3, 5)
REDUCE_ORDER = (4, 2, 6, 0, 3, 5, 1, 7)


def pick(index, values):
    result = jnp.int32(values[-1])
    for place in range(len(values) - 1):
        result = jnp.where(index == place, jnp.int32(values[place]), result)
    return result


def step_kernel(
    chosen, total, row_own, col_own, row_freq, col_freq, counts,
    own_grad, col_grad,
    cols, mine, rows, cnt, wgt, base, cells, row_logs,
    part, pair_in, send_half, recv_half, send_full, recv_full, send_z, recv_z,
    xsend_half, xrecv_half, xsend_full, xrecv_full,
    cnt_sem, ag_s, ag_r, rs_s, rs_r, x_s, x_r,
):
    r = lax.axis_index("row")
    x = lax.axis_index("col")
    k = lax.rem(r, NK)
    y = lax.rem(r // NK, NY)
    z = r // (NK * NY)
    yp, ym, y2 = lax.rem(y + 1, NY), lax.rem(y + 3, NY), lax.rem(y + 2, NY)
    xp, xm, x2 = lax.rem(x + 1, NX), lax.rem(x + 3, NX), lax.rem(x + 2, NX)
    other = 1 - k

    def dev(dx, dy, dz, dk):
        return ((dz * NY + dy) * NK + dk, dx)

    right, left = dev(x, yp, z, k), dev(x, ym, z, k)
    east, west = dev(xp, y, z, k), dev(xm, y, z, k)
    mate = dev(x, y, z, other)

    def remote(src, dst, s, q, target):
        return pltpu.make_async_remote_copy(
            src_ref=src, dst_ref=dst, send_sem=s, recv_sem=q, device_id=target, device_id_type=MESH
        )

    def count_copy(c):
        h, s, b = c // 4, (c // 2) % 2, c % 2
        lane = pl.multiple_of(lax.rem(z + h, 2) * HALF, HALF)
        return pltpu.make_async_copy(
            counts.at[s, pl.ds(b * HALF, HALF), pl.ds(lane, HALF)],
            cnt.at[s, h, pl.ds(b * HALF, HALF)],
            cnt_sem.at[c],
        )

    for c in range(8):
        count_copy(c).start()

    barrier = pltpu.get_barrier_semaphore()
    for target in (right, left, east, west, mate):
        pl.semaphore_signal(barrier, inc=1, device_id=target, device_id_type=MESH)
    for dz in range(1, NZ):
        pl.semaphore_signal(
            barrier, inc=1, device_id=dev(x, y, lax.rem(z + dz, NZ), k), device_id_type=MESH
        )
    cols[z, y, k] = col_own[...].astype(BF16)
    my_rows = pl.multiple_of(x * QUARTER, QUARTER)
    rows[pl.ds(my_rows, QUARTER)] = row_own[...].astype(BF16)
    pl.semaphore_wait(barrier, 5 + NZ - 1)

    def z_copy(i):
        zt = lax.rem(z + GATHER_ORDER[i], NZ)
        return remote(cols.at[z, y, k], cols.at[z, y, k], ag_s.at[0, i], ag_r.at[0, z], dev(x, y, zt, k))

    def z_arrival(zs):
        return remote(cols.at[zs, y, k], cols.at[zs, y, k], ag_s.at[0, 0], ag_r.at[0, zs], mate)

    def y_copy(zs, up):
        kind, target = (1, right) if up else (2, left)
        return remote(cols.at[zs, y, k], cols.at[zs, y, k], ag_s.at[kind, zs], ag_r.at[kind, zs], target)

    def y_arrival(zs, up):
        kind, src = (1, ym) if up else (2, yp)
        return remote(cols.at[zs, src, k], cols.at[zs, src, k], ag_s.at[kind, zs], ag_r.at[kind, zs], mate)

    def y_forward(zs, up):
        kind, src, start, target = (3, ym, 0, right) if up else (4, yp, PIECE // 2, left)
        ref = cols.at[zs, src, k, pl.ds(start, PIECE // 2)]
        return remote(ref, ref, ag_s.at[kind, zs], ag_r.at[kind, zs], target)

    def y_far(zs, up):
        kind, start = (3, 0) if up else (4, PIECE // 2)
        ref = cols.at[zs, y2, k, pl.ds(start, PIECE // 2)]
        return remote(ref, ref, ag_s.at[kind, zs], ag_r.at[kind, zs], mate)

    def mate_copy(zs):
        return remote(cols.at[zs, :, k], cols.at[zs, :, k], ag_s.at[5, zs], ag_r.at[5, zs], mate)

    def mate_arrival(zs):
        return remote(cols.at[zs, :, other], cols.at[zs, :, other], ag_s.at[5, zs], ag_r.at[5, zs], mate)

    def quarter(q, start, size):
        return rows.at[pl.ds(pl.multiple_of(q * QUARTER + start, 128), size)]

    def x_copy(i):
        n = 128
        q, start, target = ((x, 0, east), (x, n, west), (x, n, east), (x, 0, west), (xm, 0, east), (xp, n, west))[i]
        return remote(quarter(q, start, n), quarter(q, start, n), x_s.at[i], x_r.at[i], target)

    def x_arrival(i):
        n = 128
        q, start = ((xm, 0), (xp, n), (xm, n), (xp, 0), (x2, 0), (x2, n))[i]
        return remote(quarter(q, start, n), quarter(q, start, n), x_s.at[i], x_r.at[i], mate)

    y_copy(z, True).start()
    y_copy(z, False).start()
    for i in range(1, NZ):
        z_copy(i).start()
    for i in range(4):
        x_copy(i).start()

    logs = jnp.log(row_freq[...].astype(F32)) - total[0]
    row_logs[...] = jnp.broadcast_to(logs, (128, BLOCK)).T

    def of_block(block, options):
        result = options[3]
        for b in range(3):
            result = lax.select(block == b, options[b], result)
        return result

    def prepare(c):
        h, s = c // 4, lax.rem(c // 2, 2)
        first = lax.rem(c, 2) * HALF
        ref = cnt.at[s, h, pl.ds(first, HALF)]
        pltpu.make_async_copy(ref, ref, cnt_sem.at[c]).wait()
        parity = lax.rem(z + h, 2)
        freq = of_block(
            chosen[s],
            [col_freq[:, pl.ds(pl.multiple_of(b * BLOCK + parity * HALF, HALF), HALF)] for b in range(4)],
        )
        col_logs = jnp.log(freq.astype(F32))

        def tile(n, _):
            at = pl.ds(pl.multiple_of(first + n * PIECE, PIECE), PIECE)
            rl = row_logs[at]
            for lane in range(0, HALF, 128):
                count = cnt[s, h, at, lane : lane + 128]
                full = count > 0
                value = jnp.maximum(count, 1).astype(F32)
                root = value * lax.rsqrt(value)
                base[s, h, at, lane : lane + 128] = (rl + col_logs[:, lane : lane + 128]) - jnp.log(value)
                wgt[s, h, at, lane : lane + 128] = jnp.where(
                    full, (0.1 / BLOCK) + (0.25 / BLOCK) * root, 0.0
                )
            return 0

        lax.fori_loop(0, HALF // PIECE, tile, 0)

    def cell_tile(h, n):
        s, q = n // 2, lax.rem(n, 2)
        parity = lax.rem(z + h, 2)
        col_tile = of_block(
            chosen[s], [cols[2 * b + parity, pl.ds(2 * q, 2)].reshape(QUARTER, D) for b in range(4)]
        )
        mine[s, h, q] = col_tile
        lane = pl.multiple_of(q * QUARTER, QUARTER)
        for m in range(4):
            at = pl.ds(m * QUARTER, QUARTER)
            predicted = lax.dot_general(
                rows[at], col_tile, (((1,), (1,)), ((), ())), preferred_element_type=F32
            )
            shifted = predicted + base[s, h, at, pl.ds(lane, QUARTER)]
            w = wgt[s, h, at, pl.ds(lane, QUARTER)]
            hinge = 1.0 / (BLOCK + BLOCK * jnp.exp(-shifted))
            cells[s, h, at, pl.ds(lane, QUARTER)] = jnp.where(w > 0.0, w * shifted, hinge).astype(BF16)

    def gather_step(i, _):
        @pl.when(i < 8)
        def _():
            zs = lax.rem(z + pick(i, GATHER_ORDER), NZ)

            @pl.when(i > 0)
            def _():
                z_arrival(zs).wait_recv()
                y_copy(zs, True).start()
                y_copy(zs, False).start()

        @pl.when((i >= 1) & (i < 9))
        def _():
            zs = lax.rem(z + pick(i - 1, GATHER_ORDER), NZ)
            y_arrival(zs, True).wait_recv()
            y_forward(zs, True).start()
            y_arrival(zs, False).wait_recv()
            y_forward(zs, False).start()

        @pl.when((i >= 2) & (i < 10))
        def _():
            zs = lax.rem(z + pick(i - 2, GATHER_ORDER), NZ)
            y_far(zs, True).wait_recv()
            y_far(zs, False).wait_recv()
            mate_copy(zs).start()

        @pl.when(i == 2)
        def _():
            for j in range(2):
                x_arrival(j).wait_recv()
                x_copy(4 + j).start()

        @pl.when(i < 4)
        def _():
            prepare(2 * i)
            prepare(2 * i + 1)

        @pl.when(i == 6)
        def _():
            for j in range(2, 6):
                x_arrival(j).wait_recv()
            for j in range(4):
                mate_arrival(lax.rem(z + GATHER_ORDER[j], NZ)).wait_recv()

        @pl.when(i >= 6)
        def _():
            cell_tile(0, i - 6)

        return 0

    lax.fori_loop(0, 10, gather_step, 0)
    for j in range(4, 8):
        mate_arrival(lax.rem(z + GATHER_ORDER[j], NZ)).wait_recv()

    def mate_send(i):
        return remote(part.at[i, :, other], pair_in.at[i], rs_s.at[0, i], rs_r.at[0, i], mate)

    def mate_recv(i):
        return remote(pair_in.at[i], pair_in.at[i], rs_s.at[0, i], rs_r.at[0, i], mate)

    def half_copy(i, up):
        n, target = (0, right) if up else (1, left)
        return remote(send_half.at[n, i], recv_half.at[n, i], rs_s.at[1 + n, i], rs_r.at[1 + n, i], target)

    def full_copy(i, up):
        n, target = (0, right) if up else (1, left)
        return remote(send_full.at[n, i], recv_full.at[n, i], rs_s.at[3 + n, i], rs_r.at[3 + n, i], target)

    def home_copy(i):
        zt = lax.rem(z + pick(i, REDUCE_ORDER), NZ)
        return remote(send_z.at[i], recv_z.at[i], rs_s.at[5, i], rs_r.at[5, i], dev(x, y, zt, k))

    def chip_sum(i, dest):
        return part[i, dest, k] + pair_in[i, dest]

    def col_part(i):
        shift = pick(i, REDUCE_ORDER)
        zt = lax.rem(z + shift, NZ)
        h = lax.rem(shift, 2)
        b = zt // 2
        for q in range(2):
            lanes = slice(q * QUARTER, (q + 1) * QUARTER)
            cell = lax.select(chosen[1] == b, cells[1, h, :, lanes], jnp.zeros((BLOCK, QUARTER), BF16))
            found = lax.dot_general(
                lax.select(chosen[0] == b, cells[0, h, :, lanes], cell),
                rows[...],
                (((0,), (0,)), ((), ())),
                preferred_element_type=F32,
            )
            part[i, 2 * q : 2 * q + 2] = found.reshape(2, NK, PIECE, D)

    def row_part(q):
        at = pl.ds(pl.multiple_of(q * QUARTER, QUARTER), QUARTER)
        result = jnp.zeros((QUARTER, D), F32)
        for s in range(2):
            for h in range(2):
                result = result + jnp.dot(
                    cells[s, h, at], mine[s, h].reshape(HALF, D), preferred_element_type=F32
                )
        return result

    def xhalf(up):
        n, target = (0, east) if up else (1, west)
        return remote(xsend_half.at[n], xrecv_half.at[n], x_s.at[6 + n], x_r.at[6 + n], target)

    def xfull(up):
        n, target = (0, east) if up else (1, west)
        return remote(xsend_full.at[n], xrecv_full.at[n], x_s.at[8 + n], x_r.at[8 + n], target)

    lower = PIECE // 2

    def reduce_step(i, _):
        @pl.when((i >= 1) & (i < 9))
        def _():
            j = i - 1
            mate_recv(j).wait_recv()
            value = chip_sum(j, y2).astype(BF16)
            send_half[0, j] = value[:lower]
            half_copy(j, True).start()
            send_half[1, j] = value[lower:]
            half_copy(j, False).start()

        @pl.when((i >= 2) & (i < 10))
        def _():
            j = i - 2
            half_copy(j, True).wait_recv()
            value = chip_sum(j, yp)
            send_full[0, j, :lower] = (value[:lower] + recv_half[0, j].astype(F32)).astype(BF16)
            send_full[0, j, lower:] = value[lower:].astype(BF16)
            full_copy(j, True).start()
            half_copy(j, False).wait_recv()
            value = chip_sum(j, ym)
            send_full[1, j, :lower] = value[:lower].astype(BF16)
            send_full[1, j, lower:] = (value[lower:] + recv_half[1, j].astype(F32)).astype(BF16)
            full_copy(j, False).start()

        @pl.when(i >= 3)
        def _():
            j = i - 3
            full_copy(j, True).wait_recv()
            full_copy(j, False).wait_recv()
            value = chip_sum(j, y) + recv_full[0, j].astype(F32) + recv_full[1, j].astype(F32)

            @pl.when(j == 3)
            def _():
                col_grad[...] = value

            @pl.when(j != 3)
            def _():
                send_z[j] = value.astype(BF16)
                home_copy(j).start()

        @pl.when(i < 4)
        def _():
            cell_tile(1, i)

        @pl.when(i < 8)
        def _():
            col_part(i)
            mate_send(i).start()

        @pl.when(i == 4)
        def _():
            value = row_part(x2).astype(BF16)
            xsend_half[0] = value[:128]
            xsend_half[1] = value[128:]
            xhalf(True).start()
            xhalf(False).start()

        @pl.when(i == 5)
        def _():
            value = row_part(xp)
            xhalf(True).wait_recv()
            xsend_full[0, :128] = (value[:128] + xrecv_half[0].astype(F32)).astype(BF16)
            xsend_full[0, 128:] = value[128:].astype(BF16)
            xfull(True).start()

        @pl.when(i == 6)
        def _():
            value = row_part(xm)
            xhalf(False).wait_recv()
            xsend_full[1, :128] = value[:128].astype(BF16)
            xsend_full[1, 128:] = (value[128:] + xrecv_half[1].astype(F32)).astype(BF16)
            xfull(False).start()

        @pl.when(i == 7)
        def _():
            own_grad[...] = row_part(x)

        return 0

    lax.fori_loop(0, 11, reduce_step, 0)
    xfull(True).wait_recv()
    xfull(False).wait_recv()
    own_grad[...] += xrecv_full[0].astype(F32) + xrecv_full[1].astype(F32)
    for j in (0, 1, 2, 4, 5, 6, 7):
        home_copy(j).wait_recv()
        col_grad[...] += recv_z[j].astype(F32)

    for j in range(1, NZ):
        z_copy(j).wait_send()

    def drain(j, _):
        for up in (True, False):
            y_copy(j, up).wait_send()
            y_forward(j, up).wait_send()
            half_copy(j, up).wait_send()
            full_copy(j, up).wait_send()
        mate_copy(j).wait_send()
        mate_send(j).wait_send()

        @pl.when(j != 3)
        def _():
            home_copy(j).wait_send()

        return 0

    lax.fori_loop(0, NZ, drain, 0)
    for j in range(6):
        x_copy(j).wait_send()
    for up in (True, False):
        xhalf(up).wait_send()
        xfull(up).wait_send()


def gradients(row_embed, col_embed, row_freq, col_freq, block_cols, counts, log_total):
    vmem = pl.BlockSpec(memory_space=pltpu.VMEM)
    smem = pl.BlockSpec(memory_space=pltpu.SMEM)
    return pl.pallas_call(
        step_kernel,
        out_shape=(
            jax.ShapeDtypeStruct((QUARTER, D), F32),
            jax.ShapeDtypeStruct((PIECE, D), F32),
        ),
        in_specs=[smem, smem, vmem, vmem, vmem, vmem, pl.BlockSpec(memory_space=pl.ANY)],
        out_specs=(vmem, vmem),
        scratch_shapes=[
            pltpu.VMEM((NZ, NY, NK, PIECE, D), BF16),
            pltpu.VMEM((2, 2, 2, QUARTER, D), BF16),
            pltpu.VMEM((BLOCK, D), BF16),
            pltpu.VMEM((2, 2, BLOCK, HALF), jnp.int32),
            pltpu.VMEM((2, 2, BLOCK, HALF), F32),
            pltpu.VMEM((2, 2, BLOCK, HALF), F32),
            pltpu.VMEM((2, 2, BLOCK, HALF), BF16),
            pltpu.VMEM((BLOCK, 128), F32),
            pltpu.VMEM((NZ, NY, NK, PIECE, D), F32),
            pltpu.VMEM((NZ, NY, PIECE, D), F32),
            pltpu.VMEM((2, NZ, PIECE // 2, D), BF16),
            pltpu.VMEM((2, NZ, PIECE // 2, D), BF16),
            pltpu.VMEM((2, NZ, PIECE, D), BF16),
            pltpu.VMEM((2, NZ, PIECE, D), BF16),
            pltpu.VMEM((NZ, PIECE, D), BF16),
            pltpu.VMEM((NZ, PIECE, D), BF16),
            pltpu.VMEM((2, 128, D), BF16),
            pltpu.VMEM((2, 128, D), BF16),
            pltpu.VMEM((2, QUARTER, D), BF16),
            pltpu.VMEM((2, QUARTER, D), BF16),
            pltpu.SemaphoreType.DMA((8,)),
            pltpu.SemaphoreType.DMA((6, NZ)),
            pltpu.SemaphoreType.DMA((6, NZ)),
            pltpu.SemaphoreType.DMA((6, NZ)),
            pltpu.SemaphoreType.DMA((6, NZ)),
            pltpu.SemaphoreType.DMA((10,)),
            pltpu.SemaphoreType.DMA((10,)),
        ],
        compiler_params=pltpu.CompilerParams(
            collective_id=0, has_side_effects=True, vmem_limit_bytes=58 << 20
        ),
        cost_estimate=pl.CostEstimate(
            flops=8 << 30, bytes_accessed=12 << 20, transcendentals=8 << 20
        ),
        name="swivel_step",
    )(
        block_cols.reshape(2),
        log_total.reshape(1),
        row_embed,
        col_embed[0],
        row_freq.reshape(1, BLOCK),
        col_freq,
        counts[0, 0],
    )


def body(
    row_embed,
    row_accum,
    col_embed,
    col_accum,
    col_freq,
    row_freq,
    block_cols,
    counts,
    excluded,
    log_total,
):
    own_rows = row_embed.shape[0]
    col_index = lax.axis_index("col")
    row_index = lax.axis_index("row")
    own_freq = lax.dynamic_slice_in_dim(row_freq, col_index * own_rows, own_rows).astype(F32)
    row_ids = row_index * BLOCK + col_index * own_rows + jnp.arange(own_rows, dtype=jnp.int32)
    decayed = jnp.all(row_ids[:, None] != excluded[None, :], axis=1)
    freq_root = jnp.sqrt(own_freq)
    decay_coef = jnp.where(decayed, decay_rate * freq_root / (freq_root + 30.0), F32(0.0))
    own_grad, col_grad = gradients(
        row_embed, col_embed, row_freq, col_freq, block_cols, counts, log_total
    )
    full_grad = own_grad + decay_coef[:, None] * row_embed
    row_accum_new = row_accum + full_grad * full_grad
    row_embed_new = row_embed - learn_rate * full_grad / jnp.sqrt(row_accum_new)
    col_step = col_grad[None]
    col_accum_new = col_accum + col_step * col_step
    col_embed_new = col_embed - learn_rate * col_step / jnp.sqrt(col_accum_new)
    return (row_embed_new, row_accum_new, col_embed_new, col_accum_new)


def solution(mesh):
    in_specs = (
        P(("row", "col"), None),
        P(("row", "col"), None),
        P("col", "row", None),
        P("col", "row", None),
        P("col", None),
        P("row"),
        P("row", "col", None),
        P("row", "col", None, None, None),
        P(),
        P(),
    )
    out_specs = (
        P(("row", "col"), None),
        P(("row", "col"), None),
        P("col", "row", None),
        P("col", "row", None),
    )
    return jax.shard_map(body, mesh=mesh, in_specs=in_specs, out_specs=out_specs, check_vma=False)
```

time: 350 us -> 91.9 us (0.26)
  waiting for transfers between devices: 213 us -> 0 us
  Pallas kernels: 0 us -> 84.4 us
  local copies, waits for them, and re-layouts: 77.4 us -> 0.03 us
  matrix products: 21 us -> 0 us
  other arithmetic: 20.1 us -> 5.48 us
  between operations: 15.9 us -> 1.36 us
    reduce_scatter x2 -> x0, waiting for transfers between devices: 148 us -> none  [the longest x1 148 us: body(): col_grad = lax.psum_scatter(summed, 'row', scatter_dimension=0, tiled=True)]
    pallas_call x0 -> x1, Pallas kernels: none -> 84.4 us  [gradients(): pl.pallas_call(step_kernel, out_shape=(jax.ShapeDtypeStruct((QUARTER, D),...]
    all_gather x2 -> x0, waiting for transfers between devices: 65.4 us -> none  [the longest x1 57.7 us: body(): lax.all_gather(col_embed.astype(jnp.bfloat16), 'row', axis=1, tiled=True)]
    gather x2 -> x0, local copies, waits for them, and re-layouts: 33.6 us -> none  [body(): picked = jnp.take(col_parts[slot_id], offset, axis=0)]
    dot_general x6 -> x0, matrix products: 21 us -> none  [the longest x2 11.4 us: body(): lax.dot_general(block_rows, col_block, (((1,), (1,)), ((), ())), preferre...]
    scatter x1 -> x0, local copies, waits for them, and re-layouts: 19.2 us -> none  [body(): jnp.zeros((slots * block, width), jnp.bfloat16).at[target]]
    unnamed x24 -> x8, local copies, waits for them, and re-layouts: 14.9 us -> 0.03 us
    add x2 -> x1, other arithmetic: 9.92 us -> 0.01 us  [body(): row_index * BLOCK + col_index * own_rows]
  transfers between devices with their start and end apart: 4 -> 0, of which waited for: 3 -> 0; matrix products, arithmetic and copies ran while one was open for 28% -> 0% of each run, Pallas kernels for 0% -> 0%
where the time goes in v1:
time: 91.9 us; the launch traced here: 91.3 us
  Pallas kernels  84.4 us (92%)
  other arithmetic  5.48 us (6%)
  between operations  1.36 us (1%)
    pallas_call x1, Pallas kernels, gradients(): pl.pallas_call(step_kernel, out_shape=(jax.ShapeDtypeStruct((QUARTER, D),...  84.4 us
    sub x1, other arithmetic, body(): row_embed_new = row_embed - learn_rate * full_grad / jnp.sqrt(row_accum_new)  2.21 us

profile of v1, /device:TPU:32, one launch (start us, length us, event | category | flops | bytes accessed | tf_op | source)
XLA Modules:
  0.0 91.3 jit_solution(11468585346161175252)
XLA Ops:
  0.6 0.9 compare_reduce_fusion
  1.5 0.8 fusion.1
  2.9 0.0 copy-start
  3.0 0.0 copy-start.1
  3.0 0.0 copy-start.2
  3.0 0.0 copy-start.3
  3.0 84.4 %swivel_step.1 = (f32[256,512]{1,0:T(8,128)}, f32[64,512]{1,0:T(8,128)}) custom-call(s32[2]{0:T(128)} %bitcast.16, f32[1]{0:T(128)} %bitcast.12.total, f32[256,512]{1,0:T(8,128)} %row_own.1, f32[64,512]{1,0:T(8,128)} %bitcast.13, s32[1,1024]{1,0:T(1,128)} %bitcast.14, s32[1,4096]{1,0:T(1,128)} %col_freq.1, s32[2,1024,1024]{2,1,0:T(8,128)} %bitcast.15), custom_call_target="tpu_custom_call" | custom-call | flops 8589934592 | bytes 12582912 | tf_op jit(solution)/shard_map/swivel_step/pallas_call | solution.py:419
  87.4 0.0 copy-done
  87.4 0.0 copy-done.1
  87.4 2.2 %multiply_subtract_fusion = (f32[256,512]{1,0:T(8,128)}, f32[256,512]{1,0:T(8,128)}) fusion(f32[256,512]{1,0:T(8,128)S(1)} %copy-done, f32[256,512]{1,0:T(8,128)} %get-tuple-element.6, f32[256]{0:T(256)S(1)} %fusion.1, f32[256,512]{1,0:T(8,128)S(1)} %copy-done.1), kind=kLoop, calls=%fused_computation | loop fusion | flops 917504 | bytes 2622464 | tf_op jit(solution)/shard_map/sub | solution.py:499
  89.6 0.0 copy-done.2
  89.7 0.0 copy-done.3
  89.7 1.6 %fusion = (f32[1,64,512]{2,1,0:T(8,128)}, f32[1,64,512]{2,1,0:T(8,128)}) fusion(f32[1,64,512]{2,1,0:T(8,128)S(1)} %copy-done.2, f32[64,512]{1,0:T(8,128)} %get-tuple-element.7, f32[1,64,512]{2,1,0:T(8,128)S(1)} %copy-done.3), kind=kLoop, calls=%fused_computation.6 | loop fusion | flops 163840 | bytes 655360 | tf_op jit(solution)/shard_map/sub | solution.py:502
  (1 shorter events, 0.0 us)
Async XLA Ops:
  2.9 84.5 %copy-start = (f32[256,512]{1,0:T(8,128)S(1)}, f32[256,512]{1,0:T(8,128)}, u32[]{:S(2)}) copy-start(f32[256,512]{1,0:T(8,128)} %row_own.1) | copy-start | bytes 1572868
  3.0 84.5 %copy-start.1 = (f32[256,512]{1,0:T(8,128)S(1)}, f32[256,512]{1,0:T(8,128)}, u32[]{:S(2)}) copy-start(f32[256,512]{1,0:T(8,128)} %param.11) | copy-start | bytes 1572868
  3.0 86.7 %copy-start.2 = (f32[1,64,512]{2,1,0:T(8,128)S(1)}, f32[1,64,512]{2,1,0:T(8,128)}, u32[]{:S(2)}) copy-start(f32[1,64,512]{2,1,0:T(8,128)} %param.12) | copy-start | bytes 393220
  3.0 86.7 %copy-start.3 = (f32[1,64,512]{2,1,0:T(8,128)S(1)}, f32[1,64,512]{2,1,0:T(8,128)}, u32[]{:S(2)}) copy-start(f32[1,64,512]{2,1,0:T(8,128)} %param.13) | copy-start | bytes 393220
